TPU v7x, 32 devices: a whole 2x2x4 slice. The times are simulated.
32 devices in a mesh: lon: 8 (over z, y), lat: 4 (over x, core).
Axes of the slice: x: 2, y: 2, z: 4, core: 2. Of those that a mesh axis runs over, the one named last changes fastest.
Arguments:
- obs_values: bfloat16 [16384, 128], P(('lon', 'lat')), may hold values from -6 to 6
- obs_owner: int32 [16384, 1], P(('lon', 'lat')), may hold values from 0 to 7; in each aligned block of 512 rows (0 to 511, 512 to 1023, ...) at most 128 rows name the same one
- obs_cell: int32 [16384], P(('lon', 'lat')), may hold values from 0 to 2047
- obs_count: int32 [32], P(('lon', 'lat')), may hold values from 256 to 512, as said below
- obs_map: bfloat16 [128, 384], replicated, may hold values from -0.5 to 0.5
- column_mix: float32 [384, 384], replicated, may hold values from -0.3125 to 0.3125
- center: float32 [128, 512], P('lon', 'lat'), may hold values from 0.4 to 1
- neighbor: float32 [4, 128, 512], P(None, 'lon', 'lat'), may hold values from 0.08 to 0.3
Outputs:
- gradient: float32 [384, 128, 512], P(None, 'lon', 'lat')
Inputs may be any that keep to these rules, and one draw needn't show every extreme that they name: `obs_owner`: among the rows of one device at most 128 name the same longitude block, and some block is named by exactly 128 of them. `obs_count`: rows of a device past its count are not live; some device has all 512 rows live.
All inputs are finite; a program needn't handle non-finite values.
Results may differ from a plain program's by a relative error of at most 0.0029.
Values may be sent and summed in bfloat16 or wider, within the bound.
A program may use at most 64 MiB of HBM per device.

v0:
```python
import jax
import jax.numpy as jnp
from jax import lax
from jax.sharding import PartitionSpec as P

STEPS = 2


def with_halo(x, sides, width, wrap):
    for axis, dim in sides:
        size, length = (lax.axis_size(axis), x.shape[dim])
        up = [(i, (i + 1) % size) for i in range(size if wrap else size - 1)]
        down = [(j, i) for i, j in up]
        last = lax.slice_in_dim(x, length - width, length, axis=dim)
        first = lax.slice_in_dim(x, 0, width, axis=dim)
        before = lax.ppermute(last, axis, up)
        after = lax.ppermute(first, axis, down)
        x = jnp.concatenate([before, x, after], axis=dim)
    return x


def stencil(spread, middle, weights):
    return (
        middle * spread[:, 1:-1, 1:-1]
        + weights[0] * spread[:, :-2, 1:-1]
        + weights[1] * spread[:, 2:, 1:-1]
        + weights[2] * spread[:, 1:-1, :-2]
        + weights[3] * spread[:, 1:-1, 2:]
    )


def column_apply(mixing, adjoint):
    extent, lon_cells, lat_cells = adjoint.shape
    flat_cols = adjoint.reshape(extent, lon_cells * lat_cells)
    result = lax.dot_general(
        mixing,
        flat_cols,
        (((0,), (0,)), ((), ())),
        precision=lax.Precision.HIGHEST,
        preferred_element_type=jnp.float32,
    )
    return result.reshape(extent, lon_cells, lat_cells)


def on_device(obs_values, obs_owner, obs_cell, obs_count, obs_map, column_mix, center, neighbor):
    lon_count = lax.axis_size("lon")
    row_count = obs_values.shape[0]
    extent = column_mix.shape[0]
    capacity = 2 * row_count // lon_count
    slot_count = lon_count * capacity
    lon_cells, lat_cells = center.shape
    cell_count = lon_cells * lat_cells
    owners = obs_owner[:, 0]
    living = jnp.arange(row_count, dtype=jnp.int32) < obs_count[0]
    matches = (owners[:, None] == jnp.arange(lon_count, dtype=jnp.int32)[None, :]).astype(jnp.int32)
    earlier = jnp.sum(jnp.cumsum(matches, axis=0) * matches, axis=1) - 1
    target = owners * capacity + earlier
    places = jnp.where(living, obs_cell, -1)
    slot_places = (
        jnp.full((slot_count,), -1, jnp.int32).at[target].set(places).reshape(lon_count, capacity)
    )
    packed = (
        jnp.zeros((slot_count, extent), jnp.bfloat16)
        .at[target]
        .set(jnp.dot(obs_values, obs_map, preferred_element_type=jnp.float32).astype(jnp.bfloat16))
    )
    packed = packed.reshape(lon_count, capacity, extent)
    arrived, labels = (
        lax.all_to_all(packed, "lon", split_axis=0, concat_axis=0, tiled=True),
        lax.all_to_all(slot_places, "lon", split_axis=0, concat_axis=0, tiled=True),
    )
    block_rows = min(512, slot_count)
    batched = arrived.reshape(slot_count // block_rows, block_rows, extent)
    batched_places = labels.reshape(slot_count // block_rows, block_rows)
    targets = jnp.arange(cell_count, dtype=jnp.int32)

    def accumulate(running, element):
        values, places_in = element
        onehot = (places_in[:, None] == targets[None, :]).astype(jnp.bfloat16)
        update = lax.dot_general(
            values, onehot, (((0,), (0,)), ((), ())), preferred_element_type=jnp.float32
        )
        return (running + update, None)

    forcing, unused = lax.scan(
        accumulate, jnp.zeros((extent, cell_count), jnp.float32), (batched, batched_places)
    )
    adjoint = forcing.reshape(extent, lon_cells, lat_cells)
    for section in range(STEPS):
        mixed = column_apply(column_mix, adjoint)
        spread = with_halo(mixed, (("lon", 1),), 1, True)
        spread = with_halo(spread, (("lat", 2),), 1, False)
        adjoint = stencil(spread, center, neighbor)
    return adjoint


def solution(mesh):
    return jax.shard_map(
        on_device,
        mesh=mesh,
        in_specs=(
            P(("lon", "lat"), None),
            P(("lon", "lat"), None),
            P(("lon", "lat")),
            P(("lon", "lat")),
            P(),
            P(),
            P("lon", "lat"),
            P(None, "lon", "lat"),
        ),
        out_specs=P(None, "lon", "lat"),
        check_vma=False,
    )
```

profile of v0, /device:TPU:0, one launch (start us, length us, event | category | flops | bytes accessed | tf_op | source)
XLA Modules:
  0.0 136.8 jit_solution(2249607796687000426)
XLA Ops:
  0.8 1.1 reduce-window.6
  4.9 3.0 %scatter_custom_fusion.1 = s32[1024]{0:T(1024)} fusion(s32[512]{0:T(512)S(1)} %bitcast.56, s32[512]{0:T(512)S(1)} %fusion.29, s32[]{:T(128)} %constant.17.clone.1), kind=kCustom, calls=%fused_computation.52 | custom fusion | bytes 4100 | tf_op jit(solution)/shard_map/scatter | solution.py:60
  8.0 7.3 %all-to-all-start.1 = ((s32[8,1,128]{2,1,0:T(1,128)}), s32[8,1,128]{2,1,0:T(1,128)S(1)}, u32[]{:S(2)}, u32[]{:S(2)}) async-start(s32[8,1,128]{2,1,0:T(1,128)} %bitcast.9), calls=%async_computation.1 | async-start | bytes 8192 | tf_op jit(solution)/shard_map/all_to_all | solution.py:70
  15.2 1.2 convolution_convert_fusion
  16.4 3.3 %scatter_custom_fusion = bf16[1024,384]{1,0:T(8,128)(2,1)} fusion(s32[512]{0:T(512)S(1)} %bitcast.57, bf16[512,384]{1,0:T(8,128)(2,1)S(1)} %convolution_convert_fusion, bf16[]{:T(256)} %constant.14.clone.1), kind=kCustom, calls=%fused_computation.38 | custom fusion | bytes 786434 | tf_op jit(solution)/shard_map/scatter | solution.py:65
  19.8 1.9 %all-to-all-done.1 = s32[8,1,128]{2,1,0:T(1,128)S(1)} async-done(((s32[8,1,128]{2,1,0:T(1,128)}), s32[8,1,128]{2,1,0:T(1,128)S(1)}, u32[]{:S(2)}, u32[]{:S(2)}) %all-to-all-start.1) | async-done | bytes 4128 | tf_op jit(solution)/shard_map/all_to_all | solution.py:70
  21.6 4.1 %all-to-all-start = ((bf16[8,128,384]{2,1,0:T(8,128)(2,1)}), bf16[8,128,384]{2,1,0:T(8,128)(2,1)S(1)}, u32[]{:S(2)}, u32[]{:S(2)}) async-start(bf16[8,128,384]{2,1,0:T(8,128)(2,1)} %bitcast.6), calls=%async_computation | async-start | bytes 1572864 | tf_op jit(solution)/shard_map/all_to_all | solution.py:69
  26.9 18.6 %all-to-all-done = bf16[8,128,384]{2,1,0:T(8,128)(2,1)S(1)} async-done(((bf16[8,128,384]{2,1,0:T(8,128)(2,1)}), bf16[8,128,384]{2,1,0:T(8,128)(2,1)S(1)}, u32[]{:S(2)}, u32[]{:S(2)}) %all-to-all-start) | async-done | bytes 786464 | tf_op jit(solution)/shard_map/all_to_all | solution.py:69
  45.4 7.7 %while.11 = (s32[]{:T(128)}, f32[384,2048]{1,0:T(8,128)}, bf16[2,512,384]{2,1,0:T(8,128)(2,1)S(1)}, s32[2,512]{1,0:T(2,128)S(1)}, s32[]{:T(128)}, /*index=5*/s32[]{:T(128)}) while((s32[]{:T(128)}, f32[384,2048]{1,0:T(8,128)}, bf16[2,512,384]{2,1,0:T(8,128)(2,1)S(1)}, s32[2,512]{1,0:T(2,128)S(1)}, s32[]{:T(128)}, ...), condition=%wide.region_6.7_spmd.clone, body=%wide.region_5.6_spmd.clone.sunk | while | flops 807927808 | bytes 6690911 | solution.py:85
  45.4 2.9 %select_add_fusion.2 = f32[384,2048]{1,0:T(8,128)} fusion(f32[384,2048]{1,0:T(8,128)} %get-tuple-element.102, s32[512]{0:T(512)S(1)} %bitcast.52, pred[]{:T(512)S(6)} %compare.3, bf16[2,512,384]{2,1,0:T(8,128)(2,1)S(1)} %get-tuple-element.109, s32[]{:T(128)S(6)} %copy.62), kind=kOutput, calls=%fused_computation.5.clone.1 | convolution fusion | flops 807927808 | bytes 6686725 | tf_op jit(solution)/shard_map/while/body/eval_jaxpr/dot_general | solution.py:80
  48.4 4.8 %select_add_fusion.2 = f32[384,2048]{1,0:T(8,128)} fusion(f32[384,2048]{1,0:T(8,128)} %get-tuple-element.102, s32[512]{0:T(512)S(1)} %bitcast.52, pred[]{:T(512)S(6)} %compare.3, bf16[2,512,384]{2,1,0:T(8,128)(2,1)S(1)} %get-tuple-element.109, s32[]{:T(128)S(6)} %copy.62), kind=kOutput, calls=%fused_computation.5.clone.1 | convolution fusion | flops 807927808 | bytes 6686725 | tf_op jit(solution)/shard_map/while/body/eval_jaxpr/dot_general | solution.py:80
  53.2 8.5 %fusion.34 = f32[2048,384]{1,0:T(8,128)S(1)} fusion(f32[384,2048]{1,0:T(8,128)} %get-tuple-element.32, f32[384,384]{1,0:T(8,128)S(1)} %copy-done), kind=kOutput, calls=%fused_computation.60 | convolution fusion | flops 3623878656 | bytes 6881280 | tf_op jit(solution)/shard_map/dot_general | solution.py:35
  61.7 1.7 %copy-done.1 = f32[2048,384]{1,0:T(8,128)} copy-done((f32[2048,384]{1,0:T(8,128)}, f32[2048,384]{1,0:T(8,128)S(1)}, u32[]{:S(2)}) %copy-start.1) | copy-done | bytes 3145752
  63.5 2.3 %collective-permute-start.1 = (f32[384,1,128]{2,0,1:T(8,128)S(1)}, f32[384,1,128]{2,0,1:T(8,128)S(1)}, u32[]{:S(2)}, u32[]{:S(2)}) collective-permute-start(f32[384,1,128]{2,0,1:T(8,128)S(1)} %copy.57), channel_id=1, source_target_pairs={{4,0},{8,4},{12,8},{16,12},{20,16},{24,20},{28,24},{0,28},{5,1},{9... | collective-permute-start | bytes 589832 | tf_op jit(solution)/shard_map/ppermute | solution.py:17
  66.1 5.4 %copy.38 = f32[384,16,128]{0,1,2:T(8,128)} copy(f32[384,16,128]{0,2,1:T(8,128)} %bitcast.45) | data formatting | bytes 6291456 | tf_op jit(solution)/shard_map/reshape | solution.py:42
  71.7 3.7 %collective-permute-done = f32[384,1,128]{2,0,1:T(8,128)S(1)} collective-permute-done((f32[384,1,128]{2,0,1:T(8,128)S(1)}, f32[384,1,128]{2,0,1:T(8,128)S(1)}, u32[]{:S(2)}, u32[]{:S(2)}) %collective-permute-start) | collective-permute-done | bytes 196640 | tf_op jit(solution)/shard_map/ppermute | solution.py:16
  75.5 2.6 %pad_maximum_fusion = f32[384,18,128]{0,1,2:T(8,128)S(1)} fusion(f32[384,1,128]{0,1,2:T(1,128)S(1)} %copy.39, f32[384,16,128]{0,1,2:T(8,128)} %copy.38, f32[384,1,128]{0,1,2:T(1,128)S(1)} %copy.37), kind=kLoop, calls=%fused_computation.11 | loop fusion | flops 1769472 | bytes 7077888 | tf_op jit(solution)/shard_map/concatenate | solution.py:18
  78.2 1.3 collective-permute-start.3
  79.5 3.0 %collective-permute-start.2 = (f32[384,18,1]{0,1,2:T(8,128)S(1)}, f32[384,18,1]{0,1,2:T(8,128)S(1)}, u32[]{:S(2)}, u32[]{:S(2)}) collective-permute-start(f32[384,18,1]{0,1,2:T(8,128)S(1)} %get-tuple-element.60), channel_id=1, source_target_pairs={{0,1},{1,2},{2,3},{4,5},{5,6},{6,7},{8,9},{9,10},{10,11},{12,13},{... | collective-permute-start | bytes 82952 | tf_op jit(solution)/shard_map/ppermute | solution.py:16
  82.5 2.4 %copy.41 = f32[384,18,128]{0,2,1:T(8,128)} copy(f32[384,18,128]{0,1,2:T(8,128)S(1)} %pad_maximum_fusion) | data formatting | bytes 7077888 | tf_op jit(solution)/shard_map/concatenate | solution.py:18
  85.3 7.9 %fusion.16 = f32[384,16,128]{0,2,1:T(8,128)S(1)} fusion(f32[384,18,1]{0,2,1:T(1,128)S(1)} %copy.43, f32[384,18,128]{0,2,1:T(8,128)} %copy.41, f32[384,18,1]{0,2,1:T(1,128)S(1)} %copy.40, f32[384,1,128]{0,2,1:T(8,128)S(1)} %copy.36, f32[384,16,128]{0,2,1:T(8,128)} %bitcast.46, f32[384,1,128]{0,2,1:T(8,128)S(1)} %copy.34, f32[16,128]{1,0:T(8,128)S(1)} %get-tuple-element.68, ...), kind=kLoop, calls=%fused_computation.27 | loop fusion | flops 10223616 | bytes 10319872 | tf_op jit(solution)/shard_map/add | solution.py:24
  93.2 6.7 %fusion.35 = f32[2048,384]{1,0:T(8,128)S(1)} fusion(f32[384,2048]{0,1:T(8,128)S(1)} %bitcast.50, f32[384,384]{1,0:T(8,128)S(1)} %copy-done), kind=kOutput, calls=%fused_computation.61 | convolution fusion | flops 3623878656 | bytes 6881280 | tf_op jit(solution)/shard_map/dot_general | solution.py:35
  99.9 1.7 %copy-done.2 = f32[2048,384]{1,0:T(8,128)} copy-done((f32[2048,384]{1,0:T(8,128)}, f32[2048,384]{1,0:T(8,128)S(1)}, u32[]{:S(2)}) %copy-start.2) | copy-done | bytes 3145752
  101.7 1.9 %collective-permute-start.5 = (f32[384,1,128]{2,0,1:T(8,128)S(1)}, f32[384,1,128]{2,0,1:T(8,128)S(1)}, u32[]{:S(2)}, u32[]{:S(2)}) collective-permute-start(f32[384,1,128]{2,0,1:T(8,128)S(1)} %copy.59), channel_id=1, source_target_pairs={{4,0},{8,4},{12,8},{16,12},{20,16},{24,20},{28,24},{0,28},{5,1},{9... | collective-permute-start | bytes 589832 | tf_op jit(solution)/shard_map/ppermute | solution.py:17
  104.2 5.4 %copy.49 = f32[384,16,128]{0,1,2:T(8,128)} copy(f32[384,16,128]{0,2,1:T(8,128)} %bitcast.48) | data formatting | bytes 6291456 | tf_op jit(solution)/shard_map/reshape | solution.py:42
  109.7 4.6 %collective-permute-done.4 = f32[384,1,128]{2,0,1:T(8,128)S(1)} collective-permute-done((f32[384,1,128]{2,0,1:T(8,128)S(1)}, f32[384,1,128]{2,0,1:T(8,128)S(1)}, u32[]{:S(2)}, u32[]{:S(2)}) %collective-permute-start.4) | collective-permute-done | bytes 196640 | tf_op jit(solution)/shard_map/ppermute | solution.py:16
  114.5 2.6 %pad_maximum_fusion.1 = f32[384,18,128]{0,1,2:T(8,128)S(1)} fusion(f32[384,1,128]{0,1,2:T(1,128)S(1)} %copy.50, f32[384,16,128]{0,1,2:T(8,128)} %copy.49, f32[384,1,128]{0,1,2:T(1,128)S(1)} %copy.48), kind=kLoop, calls=%fused_computation.12 | loop fusion | flops 1769472 | bytes 7077888 | tf_op jit(solution)/shard_map/concatenate | solution.py:18
  117.1 1.3 collective-permute-start.7
  118.4 3.0 %collective-permute-start.6 = (f32[384,18,1]{0,1,2:T(8,128)S(1)}, f32[384,18,1]{0,1,2:T(8,128)S(1)}, u32[]{:S(2)}, u32[]{:S(2)}) collective-permute-start(f32[384,18,1]{0,1,2:T(8,128)S(1)} %get-tuple-element.58), channel_id=1, source_target_pairs={{0,1},{1,2},{2,3},{4,5},{5,6},{6,7},{8,9},{9,10},{10,11},{12,13},{... | collective-permute-start | bytes 82952 | tf_op jit(solution)/shard_map/ppermute | solution.py:16
  121.4 2.4 %copy.52 = f32[384,18,128]{0,2,1:T(8,128)} copy(f32[384,18,128]{0,1,2:T(8,128)S(1)} %pad_maximum_fusion.1) | data formatting | bytes 7077888 | tf_op jit(solution)/shard_map/concatenate | solution.py:18
  124.2 9.1 %fusion.8 = f32[384,16,128]{0,2,1:T(8,128)} fusion(f32[384,18,1]{0,2,1:T(1,128)S(1)} %copy.54, f32[384,18,128]{0,2,1:T(8,128)} %copy.52, f32[384,18,1]{0,2,1:T(1,128)S(1)} %copy.51, f32[384,1,128]{0,2,1:T(8,128)S(1)} %copy.47, f32[384,16,128]{0,2,1:T(8,128)} %bitcast.49, f32[384,1,128]{0,2,1:T(8,128)S(1)} %copy.45, f32[16,128]{1,0:T(8,128)S(1)} %get-tuple-element.68, ...), kind=kLoop, calls=%fused_computation.15 | loop fusion | flops 10223616 | bytes 10319872 | tf_op jit(solution)/shard_map/add | solution.py:24
  133.3 3.5 %copy.55 = f32[384,16,128]{2,1,0:T(8,128)} copy(f32[384,16,128]{0,2,1:T(8,128)} %fusion.8) | data formatting | bytes 6291456 | tf_op jit(solution)/shard_map/add | solution.py:24
  (51 shorter events, 6.9 us)
Async XLA Ops:
  0.0 53.2 %copy-start = (f32[384,384]{1,0:T(8,128)S(1)}, f32[384,384]{1,0:T(8,128)}, u32[]{:S(2)}) copy-start(f32[384,384]{1,0:T(8,128)} %param.15) | copy-start | bytes 1769476
  8.0 13.7 %all-to-all-start.1 = ((s32[8,1,128]{2,1,0:T(1,128)}), s32[8,1,128]{2,1,0:T(1,128)S(1)}, u32[]{:S(2)}, u32[]{:S(2)}) async-start(s32[8,1,128]{2,1,0:T(1,128)} %bitcast.9), calls=%async_computation.1 | async-start | bytes 8192 | tf_op jit(solution)/shard_map/all_to_all | solution.py:70
  21.6 23.8 %all-to-all-start = ((bf16[8,128,384]{2,1,0:T(8,128)(2,1)}), bf16[8,128,384]{2,1,0:T(8,128)(2,1)S(1)}, u32[]{:S(2)}, u32[]{:S(2)}) async-start(bf16[8,128,384]{2,1,0:T(8,128)(2,1)} %bitcast.6), calls=%async_computation | async-start | bytes 1572864 | tf_op jit(solution)/shard_map/all_to_all | solution.py:69
  61.6 1.7 %copy-start.1 = (f32[2048,384]{1,0:T(8,128)}, f32[2048,384]{1,0:T(8,128)S(1)}, u32[]{:S(2)}) copy-start(f32[2048,384]{1,0:T(8,128)S(1)} %fusion.34) | copy-start | bytes 9437188
  63.5 8.0 %collective-permute-start.1 = (f32[384,1,128]{2,0,1:T(8,128)S(1)}, f32[384,1,128]{2,0,1:T(8,128)S(1)}, u32[]{:S(2)}, u32[]{:S(2)}) collective-permute-start(f32[384,1,128]{2,0,1:T(8,128)S(1)} %copy.57), channel_id=1, source_target_pairs={{4,0},{8,4},{12,8},{16,12},{20,16},{24,20},{28,24},{0,28},{5,1},{9... | collective-permute-start | bytes 589832 | tf_op jit(solution)/shard_map/ppermute | solution.py:17
  65.9 9.5 %collective-permute-start = (f32[384,1,128]{2,0,1:T(8,128)S(1)}, f32[384,1,128]{2,0,1:T(8,128)S(1)}, u32[]{:S(2)}, u32[]{:S(2)}) collective-permute-start(f32[384,1,128]{2,0,1:T(8,128)S(1)} %copy.56), channel_id=1, source_target_pairs={{0,4},{4,8},{8,12},{12,16},{16,20},{20,24},{24,28},{28,0},{1,5},{5... | collective-permute-start | bytes 589832 | tf_op jit(solution)/shard_map/ppermute | solution.py:16
  75.5 7.0 %copy-start.4 = (f32[4,16,128]{2,1,0:T(8,128)S(1)}, f32[4,16,128]{2,1,0:T(8,128)}, u32[]{:S(2)}) copy-start(f32[4,16,128]{2,1,0:T(8,128)} %param.17) | copy-start | bytes 98308
  78.2 7.0 %collective-permute-start.3 = (f32[384,18,1]{0,1,2:T(8,128)S(1)}, f32[384,18,1]{0,1,2:T(8,128)S(1)}, u32[]{:S(2)}, u32[]{:S(2)}) collective-permute-start(f32[384,18,1]{0,1,2:T(8,128)S(1)} %get-tuple-element.61), channel_id=1, source_target_pairs={{1,0},{2,1},{3,2},{5,4},{6,5},{7,6},{9,8},{10,9},{11,10},{13,12},{... | collective-permute-start | bytes 82952 | tf_op jit(solution)/shard_map/ppermute | solution.py:17
  79.5 5.8 %collective-permute-start.2 = (f32[384,18,1]{0,1,2:T(8,128)S(1)}, f32[384,18,1]{0,1,2:T(8,128)S(1)}, u32[]{:S(2)}, u32[]{:S(2)}) collective-permute-start(f32[384,18,1]{0,1,2:T(8,128)S(1)} %get-tuple-element.60), channel_id=1, source_target_pairs={{0,1},{1,2},{2,3},{4,5},{5,6},{6,7},{8,9},{9,10},{10,11},{12,13},{... | collective-permute-start | bytes 82952 | tf_op jit(solution)/shard_map/ppermute | solution.py:16
  82.5 2.8 %copy-start.3 = (f32[16,128]{1,0:T(8,128)S(1)}, f32[16,128]{1,0:T(8,128)}, u32[]{:S(2)}) copy-start(f32[16,128]{1,0:T(8,128)} %param.16) | copy-start | bytes 24580
  99.9 1.7 %copy-start.2 = (f32[2048,384]{1,0:T(8,128)}, f32[2048,384]{1,0:T(8,128)S(1)}, u32[]{:S(2)}) copy-start(f32[2048,384]{1,0:T(8,128)S(1)} %fusion.35) | copy-start | bytes 9437188
  101.7 7.8 %collective-permute-start.5 = (f32[384,1,128]{2,0,1:T(8,128)S(1)}, f32[384,1,128]{2,0,1:T(8,128)S(1)}, u32[]{:S(2)}, u32[]{:S(2)}) collective-permute-start(f32[384,1,128]{2,0,1:T(8,128)S(1)} %copy.59), channel_id=1, source_target_pairs={{4,0},{8,4},{12,8},{16,12},{20,16},{24,20},{28,24},{0,28},{5,1},{9... | collective-permute-start | bytes 589832 | tf_op jit(solution)/shard_map/ppermute | solution.py:17
  103.7 10.6 %collective-permute-start.4 = (f32[384,1,128]{2,0,1:T(8,128)S(1)}, f32[384,1,128]{2,0,1:T(8,128)S(1)}, u32[]{:S(2)}, u32[]{:S(2)}) collective-permute-start(f32[384,1,128]{2,0,1:T(8,128)S(1)} %copy.58), channel_id=1, source_target_pairs={{0,4},{4,8},{8,12},{12,16},{16,20},{20,24},{24,28},{28,0},{1,5},{5... | collective-permute-start | bytes 589832 | tf_op jit(solution)/shard_map/ppermute | solution.py:16
  117.1 7.0 %collective-permute-start.7 = (f32[384,18,1]{0,1,2:T(8,128)S(1)}, f32[384,18,1]{0,1,2:T(8,128)S(1)}, u32[]{:S(2)}, u32[]{:S(2)}) collective-permute-start(f32[384,18,1]{0,1,2:T(8,128)S(1)} %get-tuple-element.59), channel_id=1, source_target_pairs={{1,0},{2,1},{3,2},{5,4},{6,5},{7,6},{9,8},{10,9},{11,10},{13,12},{... | collective-permute-start | bytes 82952 | tf_op jit(solution)/shard_map/ppermute | solution.py:17
  118.4 5.7 %collective-permute-start.6 = (f32[384,18,1]{0,1,2:T(8,128)S(1)}, f32[384,18,1]{0,1,2:T(8,128)S(1)}, u32[]{:S(2)}, u32[]{:S(2)}) collective-permute-start(f32[384,18,1]{0,1,2:T(8,128)S(1)} %get-tuple-element.58), channel_id=1, source_target_pairs={{0,1},{1,2},{2,3},{4,5},{5,6},{6,7},{8,9},{9,10},{10,11},{12,13},{... | collective-permute-start | bytes 82952 | tf_op jit(solution)/shard_map/ppermute | solution.py:16
where the time goes:
time: 138 us; the launch traced here: 137 us
  local copies, waits for them, and re-layouts  31.3 us (23%)
  waiting for transfers between devices  28.8 us (21%)
  other arithmetic  26.8 us (19%)
  starting transfers between devices  25 us (18%)
  matrix products  24.1 us (17%)
    all_to_all x1, waiting for transfers between devices, on_device(): lax.all_to_all(packed, 'lon', split_axis=0, concat_axis=0, tiled=True)  18.6 us
    add x2, other arithmetic, stencil(): middle * spread[:, 1:-1, 1:-1] + weights[0] * spread[:, :-2, 1:-1]  17 us
    dot_general x2, matrix products, column_apply(): lax.dot_general(mixing, flat_cols, (((0,), (0,)), ((), ())), precision=la...  15.2 us
    reshape x2, local copies, waits for them, and re-layouts, column_apply(): return result.reshape(extent, lon_cells, lat_cells)  10.7 us
    ppermute x4, waiting for transfers between devices, with_halo(): before = lax.ppermute(last, axis, up)  8.29 us
    dot_general x2, matrix products, accumulate(): lax.dot_general(values, onehot, (((0,), (0,)), ((), ())), preferred_eleme...  7.72 us
    all_to_all x1, starting transfers between devices, on_device(): lax.all_to_all(slot_places, 'lon', split_axis=0, concat_axis=0, tiled=True)  7.28 us
    ppermute x4, starting transfers between devices, with_halo(): before = lax.ppermute(last, axis, up)  6.79 us
  transfers between devices with their start and end apart: 10, of which 4 were waited for; matrix products, arithmetic and copies ran while one was open for 16% of the time, Pallas kernels for 0%

commit v1 on v0

v1 whole, which is shorter than its diff:
```python
import functools

import jax
import jax.numpy as jnp
from jax import lax
from jax.experimental import pallas as pl
from jax.experimental.pallas import tpu as pltpu
from jax.sharding import PartitionSpec as P

STEPS = 2
MESH = pl.DeviceIdType.MESH
HIGHEST = lax.Precision.HIGHEST
NT = (((1,), (1,)), ((), ()))
BF16 = jnp.bfloat16
F32 = jnp.float32


def with_halo(x, sides, width, wrap):
    for axis, dim in sides:
        size, length = (lax.axis_size(axis), x.shape[dim])
        up = [(i, (i + 1) % size) for i in range(size if wrap else size - 1)]
        down = [(j, i) for i, j in up]
        last = lax.slice_in_dim(x, length - width, length, axis=dim)
        first = lax.slice_in_dim(x, 0, width, axis=dim)
        before = lax.ppermute(last, axis, up)
        after = lax.ppermute(first, axis, down)
        x = jnp.concatenate([before, x, after], axis=dim)
    return x


def stencil(spread, middle, weights):
    return (
        middle * spread[:, 1:-1, 1:-1]
        + weights[0] * spread[:, :-2, 1:-1]
        + weights[1] * spread[:, 2:, 1:-1]
        + weights[2] * spread[:, 1:-1, :-2]
        + weights[3] * spread[:, 1:-1, 2:]
    )


def plain(obs_values, obs_owner, obs_cell, obs_count, obs_map, column_mix, center, neighbor):
    lon_count = lax.axis_size("lon")
    rows, width = obs_values.shape
    capacity = 2 * rows // lon_count
    slots = lon_count * capacity
    lon_cells, lat_cells = center.shape
    owners = obs_owner[:, 0]
    living = jnp.arange(rows, dtype=jnp.int32) < obs_count[0]
    number = jnp.arange(rows, dtype=jnp.int32)
    same = (owners[:, None] == owners[None, :]) & (number[None, :] < number[:, None])
    earlier = jnp.sum(same.astype(jnp.int32), axis=1)
    target = jnp.where(living, owners * capacity + earlier, -1)
    chosen = jnp.arange(slots, dtype=jnp.int32)[:, None] == target[None, :]
    packed = jnp.dot(chosen.astype(BF16), obs_values, preferred_element_type=F32).astype(BF16)
    places = jnp.sum(jnp.where(chosen, obs_cell[None, :] + 1, 0), axis=1) - 1
    packed = packed.reshape(lon_count, capacity, width)
    places = places.reshape(lon_count, capacity)
    packed = lax.all_to_all(packed, "lon", split_axis=0, concat_axis=0, tiled=True)
    places = lax.all_to_all(places, "lon", split_axis=0, concat_axis=0, tiled=True)
    cells = jnp.arange(lon_cells * lat_cells, dtype=jnp.int32)
    onehot = (places.reshape(slots)[:, None] == cells[None, :]).astype(BF16)
    adjoint = lax.dot_general(
        packed.reshape(slots, width), onehot, (((0,), (0,)), ((), ())), preferred_element_type=F32
    ).reshape(width, lon_cells, lat_cells)
    weight = obs_map.astype(F32)
    for section in range(STEPS):
        weight = jnp.dot(weight, column_mix, precision=HIGHEST)
        spread = with_halo(adjoint, (("lon", 1),), 1, True)
        spread = with_halo(spread, (("lat", 2),), 1, False)
        adjoint = stencil(spread, center, neighbor)
    return jnp.einsum("vb,vij->bij", weight, adjoint, precision=HIGHEST)


def iota(shape, dim):
    return lax.broadcasted_iota(jnp.int32, shape, dim)


def onehot_of(labels, count):
    return jnp.where(iota((count, labels.shape[1]), 0) == labels, 1.0, 0.0).astype(BF16)


def route_kernel(
    lon_n, lat_n,
    values, owner, cell, count, obs_map, mix, center, neighbor,
    f_out, halo_out, edge_out, corner_out, wlon_out, wlat_out, weight_out,
    send, recv, fsend, halo, esend, edge, corner, wlon_send, wlon, wlat_send, wlat,
    a_send, a_recv, h_send, h_recv,
):
    me, band = lax.axis_index("lon"), lax.axis_index("lat")
    east, west = lax.rem(me + 1, lon_n), lax.rem(me + lon_n - 1, lon_n)
    north, south = lax.rem(band + 1, lat_n), lax.rem(band + lat_n - 1, lat_n)
    barrier = pltpu.get_barrier_semaphore()
    partners = [(lax.rem(me + k, lon_n), band) for k in range(1, lon_n)]
    partners += [(a, b) for a in (me, east, west) for b in (north, south)]
    for partner in partners:
        pl.semaphore_signal(barrier, inc=1, device_id=partner, device_id_type=MESH)

    lon_cells, lat_cells = center.shape
    rows, width = values.shape
    cap = 2 * rows // lon_n
    own, place = owner[...], cell[...]
    owned = iota((16, rows), 0) == own
    before = jnp.where(iota((rows, rows), 0) < iota((rows, rows), 1), 1.0, 0.0).astype(BF16)
    prior = jnp.dot(jnp.where(owned, 1.0, 0.0).astype(BF16), before, preferred_element_type=F32)
    position = jnp.sum(jnp.where(owned, prior, 0.0), axis=0, keepdims=True).astype(jnp.int32)
    target = jnp.where(iota((1, rows), 1) < count[0], own * cap + position, -1)
    chosen = onehot_of(target, lon_n * cap)
    i, j = place // lat_cells, place % lat_cells
    side = jnp.where(j < 2, j, jnp.where(j >= lat_cells - 2, j - (lat_cells - 4), 4))
    sub = iota((16, rows), 0)
    labels = jnp.where(
        sub == 0,
        i // 2,
        jnp.where(sub == 1, (i % 2) * lat_cells + j, jnp.where(sub == 2, side * lon_cells + i, 0)),
    ).astype(F32)
    turned = jnp.concatenate([values[...].astype(F32).T, labels], axis=0).astype(BF16)
    packed = lax.dot_general(turned, chosen, NT, preferred_element_type=F32).astype(BF16)
    for o in range(lon_n):
        send[o] = packed[:, o * cap : (o + 1) * cap]

    weights = [center[...]] + [neighbor[k] for k in range(4)]
    wlon_send[...] = jnp.zeros_like(wlon_send)
    for k in range(5):
        wlon_send[0, k : k + 1, :] = weights[k][0:1]
        wlon_send[1, k : k + 1, :] = weights[k][lon_cells - 1 : lon_cells]
    stacked = jnp.concatenate(weights + [jnp.zeros((128 - 5 * lon_cells, lat_cells), F32)], axis=0).T
    wlat_send[0] = stacked[0:8]
    wlat_send[1] = stacked[lat_cells - 8 : lat_cells]

    pl.semaphore_wait(barrier, len(partners))

    def copy(src, dst, sem_out, sem_in, device):
        return pltpu.make_async_remote_copy(
            src_ref=src, dst_ref=dst, send_sem=sem_out, recv_sem=sem_in,
            device_id=device, device_id_type=MESH,
        )

    moves = []
    for k in range(1, lon_n):
        to = lax.rem(me + k, lon_n)
        moves.append(copy(send.at[to], recv.at[k], a_send.at[k - 1], a_recv.at[k - 1], (to, band)))
        moves[-1].start()
    later = []

    def start_later(src, dst, device):
        n = len(later)
        later.append(copy(src, dst, h_send.at[n], h_recv.at[n], device))
        later[-1].start()

    start_later(wlon_send.at[1], wlon.at[0], (east, band))
    start_later(wlon_send.at[0], wlon.at[1], (west, band))
    start_later(wlat_send.at[1], wlat.at[0], (me, north))
    start_later(wlat_send.at[0], wlat.at[1], (me, south))
    recv[0] = send[me]

    weight = obs_map[...].astype(F32)
    for section in range(STEPS):
        weight = jnp.dot(weight, mix[...], precision=HIGHEST, preferred_element_type=F32)
    weight = weight.T
    high = weight.astype(BF16)
    low = (weight - high.astype(F32)).astype(BF16)
    weight_out[...] = jnp.concatenate([high, high, low], axis=1)

    for move in moves:
        move.wait()

    arrived = jnp.concatenate([recv[k, 0:width, :] for k in range(lon_n)], axis=1)
    marks = jnp.concatenate([recv[k, width : width + 16, :] for k in range(lon_n)], axis=1)
    marks = marks.astype(F32).astype(jnp.int32)
    pair, column, rim = marks[0:1], marks[1:2], marks[2:3]
    columns = onehot_of(column, 2 * lat_cells)

    def masked(p):
        return arrived * jnp.where(pair == p, 1.0, 0.0).astype(BF16)

    def spread(pairs):
        left = jnp.concatenate([masked(p) for p in pairs], axis=0)
        out = lax.dot_general(left, columns, NT, preferred_element_type=F32).astype(BF16)
        for n, p in enumerate(pairs):
            for half in range(2):
                yield 2 * p + half, out[n * width : (n + 1) * width, half * lat_cells : (half + 1) * lat_cells]

    pairs = lon_cells // 2
    for n, (at, block) in enumerate(spread((0, pairs - 1))):
        fsend[n] = block
        f_out[at] = block
    start_later(fsend.at[pl.ds(2, 2)], halo.at[pl.ds(0, 2)], (east, band))
    start_later(fsend.at[pl.ds(0, 2)], halo.at[pl.ds(2, 2)], (west, band))
    rims = onehot_of(rim, 4 * lon_cells)
    esend[...] = lax.dot_general(rims, arrived, NT, preferred_element_type=F32).astype(BF16)
    start_later(esend.at[pl.ds(32, 32)], edge.at[pl.ds(0, 32)], (me, north))
    start_later(esend.at[pl.ds(0, 32)], edge.at[pl.ds(32, 32)], (me, south))
    start_later(esend.at[pl.ds(48, 16)], corner.at[0], (east, north))
    start_later(esend.at[pl.ds(0, 16)], corner.at[1], (east, south))
    start_later(esend.at[pl.ds(48, 16)], corner.at[2], (west, north))
    start_later(esend.at[pl.ds(0, 16)], corner.at[3], (west, south))
    for at, block in spread(range(1, pairs - 1)):
        f_out[at] = block
    for move in later:
        move.wait()
    halo_out[...] = halo[...]
    edge_out[0:64] = edge[...]
    edge_out[64:80] = esend[0:16]
    edge_out[80:96] = esend[48:64]
    corner_out[...] = corner[...]
    wlon_out[...] = wlon[...]
    wlat_out[...] = wlat[...]


def apply_kernel(
    lat_n, f, halo, edge, corner, wlon, wlat, weight, center, neighbor, out, first, grid_values
):
    lon_cells, lat_cells = center.shape
    width = f.shape[1]

    @pl.when(pl.program_id(0) == 0)
    def _():
        band = lax.axis_index("lat")
        keeps = [jnp.where(band > 0, 1.0, 0.0), jnp.where(band < lat_n - 1, 1.0, 0.0)]
        rim = edge[...].astype(F32)
        south2, south1, north1, north2, inner_s, inner_n = (rim[16 * n : 16 * (n + 1)] for n in range(6))
        corners = corner[...].astype(F32)
        cws, cwn, ces, cen = corners[0, 15:16], corners[1, 15:16], corners[2, 0:1], corners[3, 0:1]

        def rim_step(turned, here, west, east, below, above):
            w = [turned[16 * k : 16 * (k + 1)] for k in range(5)]
            up = jnp.concatenate([west, here[:-1]], axis=0)
            down = jnp.concatenate([here[1:], east], axis=0)
            return w[0] * here + w[1] * up + w[2] * down + w[3] * below + w[4] * above

        tall = jnp.zeros((120, 128), F32)
        ws = jnp.concatenate([wlat[0], tall], axis=0).T[:, 7:8]
        wn = jnp.concatenate([wlat[1], tall], axis=0).T[:, 0:1]
        step_s = rim_step(ws, south1, cws, ces, south2, inner_s)
        step_n = rim_step(wn, north1, cwn, cen, inner_n, north2)
        table = jnp.concatenate(
            [south1 * keeps[0], north1 * keeps[1], step_s * keeps[0], step_n * keeps[1],
             cws * keeps[0], cwn * keeps[1], ces * keeps[0], cen * keeps[1],
             jnp.zeros((60, width), F32)], axis=0,
        ).T
        lane = iota((width, lat_cells), 1)

        def value(n):
            if n < 0:
                return halo[n + 2].astype(F32)
            return halo[n - lon_cells + 2].astype(F32) if n >= lon_cells else f[n].astype(F32)

        def weights_at(n):
            if n < 0:
                return [wlon[0, k : k + 1, :] for k in range(5)]
            if n >= lon_cells:
                return [wlon[1, k : k + 1, :] for k in range(5)]
            return [center[n : n + 1, :]] + [neighbor[k, n : n + 1, :] for k in range(4)]

        def step(n, here, west, east, s, t):
            w = weights_at(n)
            below = jnp.where(lane == 0, table[:, s : s + 1], pltpu.roll(here, 1, 1))
            above = jnp.where(lane == lat_cells - 1, table[:, t : t + 1], pltpu.roll(here, lat_cells - 1, 1))
            return w[0] * here + w[1] * west + w[2] * east + w[3] * below + w[4] * above

        for n in range(-1, lon_cells + 1):
            s, t = (64, 65) if n < 0 else (66, 67) if n >= lon_cells else (n, 16 + n)
            first[n + 1] = step(n, value(n), value(n - 1), value(n + 1), s, t)
        for n in range(lon_cells):
            done = step(n, first[n + 1], first[n], first[n + 2], 32 + n, 48 + n)
            high = done.astype(BF16)
            at = slice(n * lat_cells, (n + 1) * lat_cells)
            grid_values[0:width, at] = high
            grid_values[width : 2 * width, at] = (done - high.astype(F32)).astype(BF16)
            grid_values[2 * width : 3 * width, at] = high

    result = jnp.dot(weight[...], grid_values[...], preferred_element_type=F32)
    chunk = weight.shape[0]
    for n in range(lon_cells):
        out[pl.ds(n, chunk, stride=lon_cells), :] = result[:, n * lat_cells : (n + 1) * lat_cells]


def fast(obs_values, obs_owner, obs_cell, obs_count, obs_map, column_mix, center, neighbor):
    lon_n, lat_n = lax.axis_size("lon"), lax.axis_size("lat")
    rows, width = obs_values.shape
    extent = column_mix.shape[0]
    lon_cells, lat_cells = center.shape
    cap = 2 * rows // lon_n
    vmem, shape = pl.BlockSpec(memory_space=pltpu.VMEM), jax.ShapeDtypeStruct
    parts = pl.pallas_call(
        functools.partial(route_kernel, lon_n, lat_n),
        out_shape=[
            shape((lon_cells, width, lat_cells), BF16),
            shape((4, width, lat_cells), BF16),
            shape((96, width), BF16),
            shape((4, 16, width), BF16),
            shape((2, 8, lat_cells), F32),
            shape((2, 8, 128), F32),
            shape((extent, 3 * width), BF16),
        ],
        in_specs=[vmem] * 3 + [pl.BlockSpec(memory_space=pltpu.SMEM)] + [vmem] * 4,
        out_specs=[vmem] * 7,
        scratch_shapes=[
            pltpu.VMEM((lon_n, width + 16, cap), BF16),
            pltpu.VMEM((lon_n, width + 16, cap), BF16),
            pltpu.VMEM((4, width, lat_cells), BF16),
            pltpu.VMEM((4, width, lat_cells), BF16),
            pltpu.VMEM((64, width), BF16),
            pltpu.VMEM((64, width), BF16),
            pltpu.VMEM((4, 16, width), BF16),
            pltpu.VMEM((2, 8, lat_cells), F32),
            pltpu.VMEM((2, 8, lat_cells), F32),
            pltpu.VMEM((2, 8, 128), F32),
            pltpu.VMEM((2, 8, 128), F32),
            pltpu.SemaphoreType.DMA((lon_n - 1,)),
            pltpu.SemaphoreType.DMA((lon_n - 1,)),
            pltpu.SemaphoreType.DMA((12,)),
            pltpu.SemaphoreType.DMA((12,)),
        ],
        compiler_params=pltpu.CompilerParams(
            collective_id=0, has_side_effects=True, vmem_limit_bytes=40 * 2**20
        ),
    )(obs_values, obs_owner.reshape(1, rows), obs_cell.reshape(1, rows), obs_count, obs_map, column_mix, center, neighbor)
    f, halo, edge, corner, wlon, wlat, weight = parts
    chunk = extent // 6
    whole = [
        pl.BlockSpec(x.shape, functools.partial(lambda d, n: (0,) * d, x.ndim))
        for x in (f, halo, edge, corner, wlon, wlat)
    ]
    out = pl.pallas_call(
        functools.partial(apply_kernel, lat_n),
        grid=(extent // chunk,),
        out_shape=shape((extent * lon_cells, lat_cells), F32),
        in_specs=whole + [
            pl.BlockSpec((chunk, 3 * width), lambda n: (n, 0)),
            pl.BlockSpec(center.shape, lambda n: (0, 0)),
            pl.BlockSpec(neighbor.shape, lambda n: (0, 0, 0)),
        ],
        out_specs=pl.BlockSpec((chunk * lon_cells, lat_cells), lambda n: (n, 0)),
        scratch_shapes=[
            pltpu.VMEM((lon_cells + 2, width, lat_cells), F32),
            pltpu.VMEM((3 * width, lon_cells * lat_cells), BF16),
        ],
        compiler_params=pltpu.CompilerParams(vmem_limit_bytes=40 * 2**20),
    )(*parts, center, neighbor)
    return out.reshape(extent, lon_cells, lat_cells)


def on_device(*arrays):
    rows, width = arrays[0].shape
    lon_n = lax.axis_size("lon")
    fits = 2 * rows // lon_n == 128 and width == 128 and arrays[6].shape == (16, 128) and lon_n <= 16
    return (fast if fits else plain)(*arrays)


def solution(mesh):
    return jax.shard_map(
        on_device,
        mesh=mesh,
        in_specs=(
            P(("lon", "lat"), None),
            P(("lon", "lat"), None),
            P(("lon", "lat")),
            P(("lon", "lat")),
            P(),
            P(),
            P("lon", "lat"),
            P(None, "lon", "lat"),
        ),
        out_specs=P(None, "lon", "lat"),
        check_vma=False,
    )
```

time: 138 us -> 34.2 us (0.25)
  waiting for transfers between devices: 28.8 us -> 0 us
  Pallas kernels: 0 us -> 27.5 us
  other arithmetic: 26.8 us -> 0 us
  local copies, waits for them, and re-layouts: 31.3 us -> 5.67 us
  starting transfers between devices: 25 us -> 0 us
  matrix products: 24.1 us -> 0 us
    pallas_call x0 -> x2, Pallas kernels: none -> 27.5 us  [the longest x1 20.7 us: fast(): pl.pallas_call(functools.partial(route_kernel, lon_n, lat_n), out_shape=[...]
    dot_general x5 -> x0, matrix products: 24.1 us -> none  [the longest x2 15.2 us: column_apply(): lax.dot_general(mixing, flat_cols, (((0,), (0,)), ((), ())), precision=la...]
    all_to_all x2 -> x0, waiting for transfers between devices: 20.5 us -> none  [the longest x1 18.6 us: on_device(): lax.all_to_all(packed, 'lon', split_axis=0, concat_axis=0, tiled=True)]
    add x2 -> x0, other arithmetic: 17 us -> none  [stencil(): middle * spread[:, 1:-1, 1:-1] + weights[0] * spread[:, :-2, 1:-1]]
    ppermute x8 -> x0, starting transfers between devices: 13.5 us -> none  [the longest x4 6.79 us: with_halo(): before = lax.ppermute(last, axis, up)]
    all_to_all x2 -> x0, starting transfers between devices: 11.4 us -> none  [the longest x1 7.28 us: on_device(): lax.all_to_all(slot_places, 'lon', split_axis=0, concat_axis=0, tiled=True)]
    reshape x3 -> x0, local copies, waits for them, and re-layouts: 10.7 us -> none  [the longest x2 10.7 us: column_apply(): return result.reshape(extent, lon_cells, lat_cells)]
    ppermute x8 -> x0, waiting for transfers between devices: 8.3 us -> none  [the longest x4 8.29 us: with_halo(): before = lax.ppermute(last, axis, up)]
  transfers between devices with their start and end apart: 10 -> 0, of which waited for: 4 -> 0; matrix products, arithmetic and copies ran while one was open for 16% -> 0% of each run, Pallas kernels for 0% -> 0%
where the time goes in v1:
time: 34.2 us; the launch traced here: 33.8 us
  Pallas kernels  27.5 us (80%)
  local copies, waits for them, and re-layouts  5.67 us (17%)
  between operations  0.67 us (2%)
    pallas_call x1, Pallas kernels, fast(): pl.pallas_call(functools.partial(route_kernel, lon_n, lat_n), out_shape=[...  20.7 us
    pallas_call x1, Pallas kernels, fast(): pl.pallas_call(functools.partial(apply_kernel, lat_n), grid=(extent // ch...  6.79 us
    unnamed x14, local copies, waits for them, and re-layouts  5.67 us

profile of v1, /device:TPU:0, one launch (start us, length us, event | category | flops | bytes accessed | tf_op | source)
XLA Modules:
  0.0 33.8 jit_solution(7024141272867646525)
XLA Ops:
  0.7 0.0 copy-start
  0.7 1.1 %copy-done = f32[384,384]{1,0:T(8,128)S(1)} copy-done((f32[384,384]{1,0:T(8,128)S(1)}, f32[384,384]{1,0:T(8,128)}, u32[]{:S(2)}) %copy-start) | copy-done | bytes 589848
  1.7 0.0 copy-start.1
  1.7 0.8 %copy-done.1 = f32[4,16,128]{2,1,0:T(8,128)S(1)} copy-done((f32[4,16,128]{2,1,0:T(8,128)S(1)}, f32[4,16,128]{2,1,0:T(8,128)}, u32[]{:S(2)}) %copy-start.1) | copy-done | bytes 32792
  2.5 0.0 copy-start.2
  2.5 0.9 %copy-done.2 = bf16[512,128]{1,0:T(8,128)(2,1)S(1)} copy-done((bf16[512,128]{1,0:T(8,128)(2,1)S(1)}, bf16[512,128]{1,0:T(8,128)(2,1)}, u32[]{:S(2)}) %copy-start.2) | copy-done | bytes 131096
  3.4 0.0 copy-start.3
  3.4 0.9 %copy-done.3 = bf16[128,384]{1,0:T(8,128)(2,1)S(1)} copy-done((bf16[128,384]{1,0:T(8,128)(2,1)S(1)}, bf16[128,384]{1,0:T(8,128)(2,1)}, u32[]{:S(2)}) %copy-start.3) | copy-done | bytes 98328
  4.3 0.0 copy-start.4
  4.3 0.7 %copy-done.4 = f32[16,128]{1,0:T(8,128)S(1)} copy-done((f32[16,128]{1,0:T(8,128)S(1)}, f32[16,128]{1,0:T(8,128)}, u32[]{:S(2)}) %copy-start.4) | copy-done | bytes 8216
  5.0 0.0 copy-start.5
  5.0 0.7 %copy-done.5 = s32[512,1]{0,1:T(1,128)S(1)} copy-done((s32[512,1]{0,1:T(1,128)S(1)}, s32[512,1]{0,1:T(1,128)}, u32[]{:S(2)}) %copy-start.5) | copy-done | bytes 2072
  5.7 0.0 copy-start.6
  5.7 0.7 %copy-done.6 = s32[512]{0:T(512)S(1)} copy-done((s32[512]{0:T(512)S(1)}, s32[512]{0:T(512)}, u32[]{:S(2)}) %copy-start.6) | copy-done | bytes 2072
  6.3 20.7 %shard_map.82 = (bf16[16,128,128]{2,1,0:T(8,128)(2,1)S(1)}, bf16[4,128,128]{2,1,0:T(8,128)(2,1)S(1)}, bf16[96,128]{1,0:T(8,128)(2,1)S(1)}, bf16[4,16,128]{2,1,0:...) custom-call(bf16[512,128]{1,0:T(8,128)(2,1)S(1)} %copy-done.2, ...), custom_call_target="tpu_custom_call" | custom-call | tf_op jit(solution)/shard_map/pallas_call | solution.py:285
  27.0 6.8 %shard_map.83 = f32[6144,128]{1,0:T(8,128)} custom-call(bf16[16,128,128]{2,1,0:T(8,128)(2,1)S(1)} %get-tuple-element.12.f, bf16[4,128,128]{2,1,0:T(8,128)(2,1)S(1)} %get-tuple-element.13.halo, bf16[96,128]{1,0:T(8,128)(2,1)S(1)} %get-tuple-element.14.edge, bf16[4,16,128]{2,1,0:T(8,128)(2,1)S(1)} %get-tuple-element.15.corner, ...), custom_call_target="tpu_custom_call" | custom-call | tf_op jit(solution)/shard_map/pallas_call | solution.py:325
Async XLA Ops:
  0.7 1.1 %copy-start = (f32[384,384]{1,0:T(8,128)S(1)}, f32[384,384]{1,0:T(8,128)}, u32[]{:S(2)}) copy-start(f32[384,384]{1,0:T(8,128)} %mix.1) | copy-start | bytes 1769476
  1.7 0.8 %copy-start.1 = (f32[4,16,128]{2,1,0:T(8,128)S(1)}, f32[4,16,128]{2,1,0:T(8,128)}, u32[]{:S(2)}) copy-start(f32[4,16,128]{2,1,0:T(8,128)} %neighbor.3) | copy-start | bytes 98308
  2.5 0.9 %copy-start.2 = (bf16[512,128]{1,0:T(8,128)(2,1)S(1)}, bf16[512,128]{1,0:T(8,128)(2,1)}, u32[]{:S(2)}) copy-start(bf16[512,128]{1,0:T(8,128)(2,1)} %values.1) | copy-start | bytes 393220
  3.4 0.9 %copy-start.3 = (bf16[128,384]{1,0:T(8,128)(2,1)S(1)}, bf16[128,384]{1,0:T(8,128)(2,1)}, u32[]{:S(2)}) copy-start(bf16[128,384]{1,0:T(8,128)(2,1)} %obs_map.1) | copy-start | bytes 294916
  4.3 0.7 %copy-start.4 = (f32[16,128]{1,0:T(8,128)S(1)}, f32[16,128]{1,0:T(8,128)}, u32[]{:S(2)}) copy-start(f32[16,128]{1,0:T(8,128)} %center.3) | copy-start | bytes 24580
  5.0 0.7 %copy-start.5 = (s32[512,1]{0,1:T(1,128)S(1)}, s32[512,1]{0,1:T(1,128)}, u32[]{:S(2)}) copy-start(s32[512,1]{0,1:T(1,128)} %param.9) | copy-start | bytes 6148
  5.7 0.7 %copy-start.6 = (s32[512]{0:T(512)S(1)}, s32[512]{0:T(512)}, u32[]{:S(2)}) copy-start(s32[512]{0:T(512)} %param.10) | copy-start | bytes 6148

commit v2 on v1

--- a/solution.py
+++ b/solution.py
@@ -81,11 +81,19 @@
 
 def route_kernel(
     lon_n, lat_n,
-    values, owner, cell, count, obs_map, mix, center, neighbor,
+    values_in, owner_in, cell_in, count, obs_map_in, mix_in, center_in, neighbor_in,
     f_out, halo_out, edge_out, corner_out, wlon_out, wlat_out, weight_out,
     send, recv, fsend, halo, esend, edge, corner, wlon_send, wlon, wlat_send, wlat,
     a_send, a_recv, h_send, h_recv,
+    values, owner, cell, obs_map, mix, center, neighbor, in_sem,
 ):
+    pairs_in = [
+        (owner_in, owner), (cell_in, cell), (values_in, values), (center_in, center),
+        (neighbor_in, neighbor), (obs_map_in, obs_map), (mix_in, mix),
+    ]
+    fetches = [pltpu.make_async_copy(a, b, in_sem.at[n]) for n, (a, b) in enumerate(pairs_in)]
+    for fetch in fetches:
+        fetch.start()
     me, band = lax.axis_index("lon"), lax.axis_index("lat")
     east, west = lax.rem(me + 1, lon_n), lax.rem(me + lon_n - 1, lon_n)
     north, south = lax.rem(band + 1, lat_n), lax.rem(band + lat_n - 1, lat_n)
@@ -98,6 +106,8 @@
     lon_cells, lat_cells = center.shape
     rows, width = values.shape
     cap = 2 * rows // lon_n
+    for fetch in fetches[:3]:
+        fetch.wait()
     own, place = owner[...], cell[...]
     owned = iota((16, rows), 0) == own
     before = jnp.where(iota((rows, rows), 0) < iota((rows, rows), 1), 1.0, 0.0).astype(BF16)
@@ -118,6 +128,8 @@
     for o in range(lon_n):
         send[o] = packed[:, o * cap : (o + 1) * cap]
 
+    for fetch in fetches[3:5]:
+        fetch.wait()
     weights = [center[...]] + [neighbor[k] for k in range(4)]
     wlon_send[...] = jnp.zeros_like(wlon_send)
     for k in range(5):
@@ -153,6 +165,8 @@
     start_later(wlat_send.at[0], wlat.at[1], (me, south))
     recv[0] = send[me]
 
+    for fetch in fetches[5:]:
+        fetch.wait()
     weight = obs_map[...].astype(F32)
     for section in range(STEPS):
         weight = jnp.dot(weight, mix[...], precision=HIGHEST, preferred_element_type=F32)
@@ -282,6 +296,7 @@
     lon_cells, lat_cells = center.shape
     cap = 2 * rows // lon_n
     vmem, shape = pl.BlockSpec(memory_space=pltpu.VMEM), jax.ShapeDtypeStruct
+    hbm = pl.BlockSpec(memory_space=pltpu.HBM)
     parts = pl.pallas_call(
         functools.partial(route_kernel, lon_n, lat_n),
         out_shape=[
@@ -293,7 +308,7 @@
             shape((2, 8, 128), F32),
             shape((extent, 3 * width), BF16),
         ],
-        in_specs=[vmem] * 3 + [pl.BlockSpec(memory_space=pltpu.SMEM)] + [vmem] * 4,
+        in_specs=[hbm] * 3 + [pl.BlockSpec(memory_space=pltpu.SMEM)] + [hbm] * 4,
         out_specs=[vmem] * 7,
         scratch_shapes=[
             pltpu.VMEM((lon_n, width + 16, cap), BF16),
@@ -311,17 +326,21 @@
             pltpu.SemaphoreType.DMA((lon_n - 1,)),
             pltpu.SemaphoreType.DMA((12,)),
             pltpu.SemaphoreType.DMA((12,)),
+            pltpu.VMEM(obs_values.shape, BF16),
+            pltpu.VMEM((1, rows), jnp.int32),
+            pltpu.VMEM((1, rows), jnp.int32),
+            pltpu.VMEM(obs_map.shape, BF16),
+            pltpu.VMEM(column_mix.shape, F32),
+            pltpu.VMEM(center.shape, F32),
+            pltpu.VMEM(neighbor.shape, F32),
+            pltpu.SemaphoreType.DMA((7,)),
         ],
         compiler_params=pltpu.CompilerParams(
-            collective_id=0, has_side_effects=True, vmem_limit_bytes=40 * 2**20
+            collective_id=0, has_side_effects=True, vmem_limit_bytes=62 * 2**20
         ),
     )(obs_values, obs_owner.reshape(1, rows), obs_cell.reshape(1, rows), obs_count, obs_map, column_mix, center, neighbor)
-    f, halo, edge, corner, wlon, wlat, weight = parts
     chunk = extent // 6
-    whole = [
-        pl.BlockSpec(x.shape, functools.partial(lambda d, n: (0,) * d, x.ndim))
-        for x in (f, halo, edge, corner, wlon, wlat)
-    ]
+    whole = [pl.BlockSpec(x.shape, functools.partial(lambda d, n: (0,) * d, x.ndim)) for x in parts[:6]]
     out = pl.pallas_call(
         functools.partial(apply_kernel, lat_n),
         grid=(extent // chunk,),
@@ -336,7 +355,7 @@
             pltpu.VMEM((lon_cells + 2, width, lat_cells), F32),
             pltpu.VMEM((3 * width, lon_cells * lat_cells), BF16),
         ],
-        compiler_params=pltpu.CompilerParams(vmem_limit_bytes=40 * 2**20),
+        compiler_params=pltpu.CompilerParams(vmem_limit_bytes=62 * 2**20),
     )(*parts, center, neighbor)
     return out.reshape(extent, lon_cells, lat_cells)
 

time: 34.2 us -> 31.3 us (0.915)
  local copies, waits for them, and re-layouts: 5.67 us -> 0 us
  Pallas kernels: 27.5 us -> 30.2 us
    unnamed x14 -> x0, local copies, waits for them, and re-layouts: 5.67 us -> none
    pallas_call x1, Pallas kernels: 6.79 us -> 8.43 us  [fast(): pl.pallas_call(functools.partial(apply_kernel, lat_n), grid=(extent // ch...]
    pallas_call x1, Pallas kernels: 20.7 us -> 21.8 us  [fast(): pl.pallas_call(functools.partial(route_kernel, lon_n, lat_n), out_shape=[...]
where the time goes in v2:
time: 31.3 us; the launch traced here: 30.9 us
  Pallas kernels  30.2 us (96%)
  between operations  0.66 us (2%)
    pallas_call x1, Pallas kernels, fast(): pl.pallas_call(functools.partial(route_kernel, lon_n, lat_n), out_shape=[...  21.8 us
    pallas_call x1, Pallas kernels, fast(): pl.pallas_call(functools.partial(apply_kernel, lat_n), grid=(extent // ch...  8.43 us

profile of v2, /device:TPU:0, one launch (start us, length us, event | category | flops | bytes accessed | tf_op | source)
XLA Modules:
  0.0 30.9 jit_solution(13976330848745853645)
XLA Ops:
  0.7 21.8 %shard_map.82 = (bf16[16,128,128]{2,1,0:T(8,128)(2,1)}, bf16[4,128,128]{2,1,0:T(8,128)(2,1)}, bf16[96,128]{1,0:T(8,128)(2,1)}, bf16[4,16,128]{2,1,0:T(8,128)(2,1...) custom-call(bf16[512,128]{1,0:T(8,128)(2,1)} %values_in.1, s32[1,512]{1,0:T(1,128)} %bitcast.3, ...), custom_call_target="tpu_custom_call" | custom-call | tf_op jit(solution)/shard_map/pallas_call | solution.py:300
  22.5 8.4 %shard_map.83 = f32[6144,128]{1,0:T(8,128)} custom-call(bf16[16,128,128]{2,1,0:T(8,128)(2,1)} %get-tuple-element.12.f, bf16[4,128,128]{2,1,0:T(8,128)(2,1)} %get-tuple-element.13.halo, bf16[96,128]{1,0:T(8,128)(2,1)} %get-tuple-element.14.edge, bf16[4,16,128]{2,1,0:T(8,128)(2,1)} %get-tuple-element.15.corner, f32[2,8,128]{2,1,0:T(8,128)} %get-tuple-element.16.wlon, ...), custom_call_target="tpu_custom_call" | custom-call | tf_op jit(solution)/shard_map/pallas_call | solution.py:344

commit v3 on v2

--- a/solution.py
+++ b/solution.py
@@ -339,7 +339,7 @@
             collective_id=0, has_side_effects=True, vmem_limit_bytes=62 * 2**20
         ),
     )(obs_values, obs_owner.reshape(1, rows), obs_cell.reshape(1, rows), obs_count, obs_map, column_mix, center, neighbor)
-    chunk = extent // 6
+    chunk = extent // 3
     whole = [pl.BlockSpec(x.shape, functools.partial(lambda d, n: (0,) * d, x.ndim)) for x in parts[:6]]
     out = pl.pallas_call(
         functools.partial(apply_kernel, lat_n),

time: 31.3 us -> 29.6 us (0.946)
  Pallas kernels: 30.2 us -> 28.8 us
    pallas_call x1, Pallas kernels: 8.43 us -> 6.95 us  [fast(): pl.pallas_call(functools.partial(apply_kernel, lat_n), grid=(extent // ch...]
where the time goes in v3:
time: 29.6 us; the launch traced here: 29.4 us
  Pallas kernels  28.8 us (97%)
  between operations  0.66 us (2%)
    pallas_call x1, Pallas kernels, fast(): pl.pallas_call(functools.partial(route_kernel, lon_n, lat_n), out_shape=[...  21.8 us
    pallas_call x1, Pallas kernels, fast(): pl.pallas_call(functools.partial(apply_kernel, lat_n), grid=(extent // ch...  6.95 us

profile of v3, /device:TPU:0, one launch (start us, length us, event | category | flops | bytes accessed | tf_op | source)
XLA Modules:
  0.0 29.4 jit_solution(6254354918052823090)
XLA Ops:
  0.7 21.8 %shard_map.82 = (bf16[16,128,128]{2,1,0:T(8,128)(2,1)}, bf16[4,128,128]{2,1,0:T(8,128)(2,1)}, bf16[96,128]{1,0:T(8,128)(2,1)}, bf16[4,16,128]{2,1,0:T(8,128)(2,1...) custom-call(bf16[512,128]{1,0:T(8,128)(2,1)} %values_in.1, s32[1,512]{1,0:T(1,128)} %bitcast.3, ...), custom_call_target="tpu_custom_call" | custom-call | tf_op jit(solution)/shard_map/pallas_call | solution.py:300
  22.5 7.0 %shard_map.83 = f32[6144,128]{1,0:T(8,128)} custom-call(bf16[16,128,128]{2,1,0:T(8,128)(2,1)} %get-tuple-element.12.f, bf16[4,128,128]{2,1,0:T(8,128)(2,1)} %get-tuple-element.13.halo, bf16[96,128]{1,0:T(8,128)(2,1)} %get-tuple-element.14.edge, bf16[4,16,128]{2,1,0:T(8,128)(2,1)} %get-tuple-element.15.corner, f32[2,8,128]{2,1,0:T(8,128)} %get-tuple-element.16.wlon, ...), custom_call_target="tpu_custom_call" | custom-call | tf_op jit(solution)/shard_map/pallas_call | solution.py:344

commit v4 on v3

--- a/solution.py
+++ b/solution.py
@@ -339,7 +339,7 @@
             collective_id=0, has_side_effects=True, vmem_limit_bytes=62 * 2**20
         ),
     )(obs_values, obs_owner.reshape(1, rows), obs_cell.reshape(1, rows), obs_count, obs_map, column_mix, center, neighbor)
-    chunk = extent // 3
+    chunk = extent // 2
     whole = [pl.BlockSpec(x.shape, functools.partial(lambda d, n: (0,) * d, x.ndim)) for x in parts[:6]]
     out = pl.pallas_call(
         functools.partial(apply_kernel, lat_n),

time: 29.6 us -> 29.2 us (0.986)
  Pallas kernels: 28.8 us -> 28.4 us
    pallas_call x1, Pallas kernels: 6.95 us -> 6.55 us  [fast(): pl.pallas_call(functools.partial(apply_kernel, lat_n), grid=(extent // ch...]
where the time goes in v4:
time: 29.2 us; the launch traced here: 29 us
  Pallas kernels  28.4 us (97%)
  between operations  0.66 us (2%)
    pallas_call x1, Pallas kernels, fast(): pl.pallas_call(functools.partial(route_kernel, lon_n, lat_n), out_shape=[...  21.8 us
    pallas_call x1, Pallas kernels, fast(): pl.pallas_call(functools.partial(apply_kernel, lat_n), grid=(extent // ch...  6.55 us

profile of v4, /device:TPU:0, one launch (start us, length us, event | category | flops | bytes accessed | tf_op | source)
XLA Modules:
  0.0 29.0 jit_solution(1560158754181644346)
XLA Ops:
  0.7 21.8 %shard_map.82 = (bf16[16,128,128]{2,1,0:T(8,128)(2,1)}, bf16[4,128,128]{2,1,0:T(8,128)(2,1)}, bf16[96,128]{1,0:T(8,128)(2,1)}, bf16[4,16,128]{2,1,0:T(8,128)(2,1...) custom-call(bf16[512,128]{1,0:T(8,128)(2,1)} %values_in.1, s32[1,512]{1,0:T(1,128)} %bitcast.3, ...), custom_call_target="tpu_custom_call" | custom-call | tf_op jit(solution)/shard_map/pallas_call | solution.py:300
  22.5 6.6 %shard_map.83 = f32[6144,128]{1,0:T(8,128)} custom-call(bf16[16,128,128]{2,1,0:T(8,128)(2,1)} %get-tuple-element.12.f, bf16[4,128,128]{2,1,0:T(8,128)(2,1)} %get-tuple-element.13.halo, bf16[96,128]{1,0:T(8,128)(2,1)} %get-tuple-element.14.edge, bf16[4,16,128]{2,1,0:T(8,128)(2,1)} %get-tuple-element.15.corner, f32[2,8,128]{2,1,0:T(8,128)} %get-tuple-element.16.wlon, ...), custom_call_target="tpu_custom_call" | custom-call | tf_op jit(solution)/shard_map/pallas_call | solution.py:344
